TPU v7x, 256 devices: a whole 4x4x8 slice. The times are simulated.
256 devices in a mesh: dp: 4 (over z_lo), cls: 64 (over y, z_hi, x, core).
Axes of the slice: x: 4, y: 4, z: 8 (z_hi: 2, z_lo: 4; z = z_hi * 4 + z_lo), core: 2. Of those that a mesh axis runs over, the one named last changes fastest.
Arguments:
- embeddings: bfloat16 [4096, 384], P(('dp', 'cls')), may hold values from -4 to 4
- cluster_ids: int32 [4096], P(('dp', 'cls')), may hold values from 0 to 131071
- prototypes: bfloat16 [384, 131072], P(None, 'cls'), may hold values from -2 to 2
Outputs:
- embed_grad: float32 [4096, 384], P(('dp', 'cls'))
- proto_grad: float32 [384, 131072], P('dp', 'cls')
All inputs are finite; a program needn't handle non-finite values.
Results may differ from a plain program's by a relative error of at most 0.00505.
Values may be sent and summed in bfloat16 or wider, within the bound.
A program may use at most 128 MiB of HBM per device.

v0:
```python
import jax
import jax.numpy as jnp
from jax import lax
from jax.sharding import PartitionSpec as P

LOGIT_SCALE = 10.0


def on_device(embeddings, cluster_ids, prototypes):
    contract_cols = (((1,), (1,)), ((), ()))
    contract_rows = (((0,), (0,)), ((), ()))
    gathered, group_ids = (
        lax.all_gather(embeddings, "cls", axis=0, tiled=True),
        lax.all_gather(cluster_ids, "cls", axis=0, tiled=True),
    )
    width = prototypes.shape[1]
    col_offset = lax.axis_index("cls") * width
    logits = jnp.dot(gathered, prototypes, preferred_element_type=jnp.float32) * LOGIT_SCALE
    row_peak = lax.pmax(jnp.max(logits, axis=1), "cls")
    exponent = jnp.exp(logits - row_peak[:, None])
    row_total = lax.psum(jnp.sum(exponent, axis=1), "cls")
    soft_probs = exponent / row_total[:, None]
    total_crops = gathered.shape[0] * lax.axis_size("dp")
    classes = width * lax.axis_size("cls")
    column_mass = lax.psum(jnp.sum(soft_probs, axis=0), "dp")
    log_ratio = jnp.log(column_mass * (classes / total_crops))
    row_dot = lax.psum(jnp.sum(soft_probs * log_ratio[None, :], axis=1), "cls")
    columns = col_offset + jnp.arange(width, dtype=jnp.int32)
    onehot = (group_ids[:, None] == columns[None, :]).astype(jnp.float32)
    grad_logit = soft_probs - onehot + soft_probs * (log_ratio[None, :] - row_dot[:, None])
    grad_narrow = grad_logit.astype(jnp.bfloat16)
    embed_grad = lax.psum_scatter(
        lax.dot_general(grad_narrow, prototypes, contract_cols, preferred_element_type=jnp.float32)
        * LOGIT_SCALE,
        "cls",
        scatter_dimension=0,
        tiled=True,
    )
    proto_grad = lax.psum_scatter(
        lax.dot_general(gathered, grad_narrow, contract_rows, preferred_element_type=jnp.float32)
        * LOGIT_SCALE,
        "dp",
        scatter_dimension=0,
        tiled=True,
    )
    return (embed_grad, proto_grad)


def solution(mesh):
    placed = (P(("dp", "cls"), None), P(("dp", "cls")), P(None, "cls"))
    return jax.shard_map(
        on_device,
        mesh=mesh,
        in_specs=placed,
        out_specs=(P(("dp", "cls"), None), P("dp", "cls")),
        check_vma=False,
    )
```

profile of v0, /device:TPU:32, one launch (start us, length us, event | category | flops | bytes accessed | tf_op | source)
XLA Modules:
  0.0 1017.6 jit_solution(10562264437511697986)
XLA Ops:
  7.2 0.0 copy-start
  7.2 0.0 reduce-scatter.5.cloned.1.call-start
  7.2 120.9 %all_gather.6 = bf16[1024,384]{1,0:T(8,128)(2,1)S(1)} all-gather(bf16[16,384]{1,0:T(8,128)(2,1)} %param.3), channel_id=1, replica_groups=mesh['dp'=4,'cls'=64] {'cls'}, dimensions={0}, use_global_device_ids=true | all-gather | bytes 798720 | tf_op jit(solution)/shard_map/all_gather | solution.py:13
  128.1 5.6 multiply_reduce_fusion.1
  133.7 201.3 %pmax.7 = f32[1024]{0:T(1024)S(1)} all-reduce(f32[1024]{0:T(1024)S(1)} %get-tuple-element.8), channel_id=1, replica_groups=mesh['dp'=4,'cls'=64] {'cls'}, use_global_device_ids=true, to_apply=%region_1.0 | all-reduce | flops 1024 | bytes 8192 | tf_op jit(solution)/shard_map/pmax | solution.py:19
  334.9 4.3 fusion.1
  339.3 201.0 %psum.21 = f32[1024]{0:T(1024)S(1)} all-reduce(f32[1024]{0:T(1024)S(1)} %fusion.1), channel_id=1, replica_groups=mesh['dp'=4,'cls'=64] {'cls'}, use_global_device_ids=true, to_apply=%region_3.0 | all-reduce | flops 1024 | bytes 8192 | tf_op jit(solution)/shard_map/psum | solution.py:21
  540.3 6.4 fusion.2
  546.8 9.4 psum.22
  556.2 4.0 multiply_reduce_fusion
  560.2 201.0 %psum.23 = f32[1024]{0:T(1024)S(1)} all-reduce(f32[1024]{0:T(1024)S(1)} %multiply_reduce_fusion), channel_id=1, replica_groups=mesh['dp'=4,'cls'=64] {'cls'}, use_global_device_ids=true, to_apply=%region_7.0 | all-reduce | flops 1024 | bytes 8192 | tf_op jit(solution)/shard_map/psum | solution.py:27
  761.1 0.6 dynamic-slice
  762.4 0.2 dynamic-update-slice
  762.6 13.3 %all-reduce = s32[1024]{0:T(1024)S(1)} all-reduce(s32[1024]{0:T(1024)S(1)} %dynamic-update-slice), channel_id=1, replica_groups=mesh['dp'=4,'cls'=64] {'cls'}, use_global_device_ids=true, to_apply=%add | all-reduce | flops 1024 | bytes 8192
  775.9 4.5 add_convert_fusion
  780.4 1.9 copy-done.1
  782.3 3.6 convolution_multiply_fusion
  785.9 0.0 reduce-scatter.5.cloned.1.call-update
  785.9 0.0 reduce-scatter.7.cloned.1.call-start
  786.0 6.3 multiply_bitcast_fusion
  792.2 3.5 copy.7
  795.8 0.0 reduce-scatter.7.cloned.1.call-update
  795.8 151.2 %reduce-scatter.5.cloned.1.call-done = f32[16,384]{1,0:T(8,128)} async-done(((f32[1024,384]{1,0:T(8,128)}), f32[16,384]{1,0:T(8,128)}) %reduce-scatter.5.cloned.1.call-update) | async-done | bytes 24592 | tf_op jit(solution)/shard_map/reduce_scatter | solution.py:32
  947.0 63.7 %reduce-scatter.7.cloned.1.call-done = f32[96,2048]{1,0:T(8,128)} async-done(((f32[384,2048]{1,0:T(8,128)}), f32[96,2048]{1,0:T(8,128)}) %reduce-scatter.7.cloned.1.call-update) | async-done | bytes 786448
  (9 shorter events, 0.0 us)
Async XLA Ops:
  7.2 120.9 %copy-start = (bf16[384,2048]{1,0:T(8,128)(2,1)S(1)}, bf16[384,2048]{1,0:T(8,128)(2,1)}, u32[]{:S(2)}) copy-start(bf16[384,2048]{1,0:T(8,128)(2,1)} %param.5) | copy-start | bytes 4718596
  7.2 939.8 %reduce-scatter.5.cloned.1.call-start = ((), (), s32[]{:S(2)}) async-start(), calls=%async_computation.2 | async-start | bytes 1597440 | tf_op jit(solution)/shard_map/reduce_scatter | solution.py:32
  546.7 214.4 %copy-start.3 = (u32[256]{0:T(256)S(1)}, u32[256]{0:T(256)}, u32[]{:S(2)}) copy-start(u32[256]{0:T(256)} %constant.20) | copy-start | bytes 3076
  546.8 215.6 %copy-start.2 = (s32[16]{0:T(128)S(1)}, s32[16]{0:T(128)}, u32[]{:S(2)}) copy-start(s32[16]{0:T(128)} %param.4) | copy-start | bytes 196
  780.4 1.9 copy-start.1
  785.9 224.8 %reduce-scatter.7.cloned.1.call-start = ((), (), s32[]{:S(2)}) async-start(), calls=%async_computation.3 | async-start | bytes 3932160
Sparse Core Ops, SparseCore 0:
  786.0 160.9 reduce-scatter.4
  950.3 60.3 reduce-scatter.6
where the time goes:
time: 1020 us
  blocking collectives  747 us (73%)
  waiting for transfers between devices  215 us (21%)
  other arithmetic  19.2 us (2%)
  matrix products  15.4 us (2%)
  between operations  14.8 us (1%)
    pmax x1, blocking collectives, on_device(): row_peak = lax.pmax(jnp.max(logits, axis=1), 'cls')  201 us
    psum x1, blocking collectives, on_device(): row_total = lax.psum(jnp.sum(exponent, axis=1), 'cls')  201 us
    psum x1, blocking collectives, on_device(): row_dot = lax.psum(jnp.sum(soft_probs * log_ratio[None, :], axis=1), 'cls')  201 us
    reduce_scatter x1, waiting for transfers between devices, on_device(): lax.psum_scatter(lax.dot_general(grad_narrow, prototypes, contract_cols,...  151 us
    all_gather x1, blocking collectives, on_device(): lax.all_gather(embeddings, 'cls', axis=0, tiled=True)  121 us
    unnamed x3, waiting for transfers between devices  63.8 us
  transfers between devices with their start and end apart: 2, of which 2 were waited for; matrix products, arithmetic and copies ran while one was open for 1% of the time, Pallas kernels for 0%

commit v1 on v0

v1 whole, which is shorter than its diff:
```python
import functools

import jax
import jax.numpy as jnp
from jax import lax
from jax.experimental import pallas as pl
from jax.experimental.pallas import tpu as pltpu
from jax.sharding import PartitionSpec as P

LOGIT_SCALE = 10.0
MESH = pl.DeviceIdType.MESH
F32 = jnp.float32
BF16 = jnp.bfloat16

D = 384
DX = 512
W = 2048
R = 1024
NC = 4
CW = W // NC
Q = D // 4
NT = (((1,), (1,)), ((), ()))
SEVEN = [(dz, da) for da in range(4) for dz in range(2) if dz or da]


def split_rows(v):
    hi = v.astype(BF16)
    r1 = v - hi.astype(F32)
    mid = r1.astype(BF16)
    lo = (r1 - mid.astype(F32)).astype(BF16)
    row = lax.broadcasted_iota(jnp.int32, (16, v.shape[1]), 0)
    zero = jnp.zeros((16, v.shape[1]), F32)
    out = jnp.where(row == 0, hi.astype(F32), zero)
    out = jnp.where(row == 1, mid.astype(F32), out)
    out = jnp.where(row == 2, lo.astype(F32), out)
    return out.astype(BF16)


def kernel(classes_over_crops, e_ref, id_ref, w_ref, eo_ref, po_ref,
           eg, pb, lb, mcol, scol, acol, ccol, icol, et, gb,
           st, ra, rb, rc, cm, qt, qa, qb, qc, pf, pp, pr,
           xe, xc, y1, xb, y2, xa,
           s_e1, r_e1, s_e2, r_e2, s_e3, r_e3,
           s_a, r_a, s_b, r_b, s_c, r_c, s_m, r_m,
           s_p, r_p, s_x1, r_x1, s_x2, r_x2, s_x3, r_x3):
    dp = lax.axis_index("dp")
    cls = lax.axis_index("cls")
    core = lax.rem(cls, 2)
    x = lax.rem(cls // 2, 4)
    zh = lax.rem(cls // 8, 2)
    y = cls // 16
    other = 1 - core
    alpha = y * other + x * core
    beta = x * other + y * core

    def at(zz, aa, bb):
        yy = aa * other + bb * core
        xx = bb * other + aa * core
        return (dp, ((yy * 2 + zz) * 4 + xx) * 2 + core)

    def add4(v, k):
        return lax.rem(v + k, 4)

    def seven(dz, da):
        return lax.rem(zh + dz, 2), add4(alpha, da)

    partner = (dp, cls + 1 - 2 * core)
    dp_peers = [(add4(dp, j), cls) for j in (1, 2, 3)]
    beta_peers = [at(zh, alpha, add4(beta, k)) for k in (1, 2, 3)]
    seven_peers = [at(*seven(dz, da), beta) for dz, da in SEVEN]

    barrier = pltpu.get_barrier_semaphore()
    everyone = [partner] + dp_peers + beta_peers + seven_peers
    for peer in everyone:
        pl.semaphore_signal(barrier, inc=1, device_id=peer, device_id_type=MESH)

    ids = id_ref[...]
    lane = lax.broadcasted_iota(jnp.int32, (16, 128), 1)
    digits = jnp.where(lane == 0, ids >> 10, jnp.where(lane == 1, (ids >> 5) & 31, jnp.where(lane == 2, ids & 31, 0)))
    eg[core, beta, zh, alpha, :, :D] = e_ref[...]
    eg[core, beta, zh, alpha, :, D:] = digits.astype(F32).astype(BF16)

    pl.semaphore_wait(barrier, len(everyone))

    def remote(src, dst, ssem, rsem, peer):
        return pltpu.make_async_remote_copy(
            src_ref=src, dst_ref=dst, send_sem=ssem, recv_sem=rsem, device_id=peer, device_id_type=MESH
        )

    mine = eg.at[core, beta, zh, alpha]
    sends = []
    for j, peer in enumerate(seven_peers):
        c = remote(mine, mine, s_e1.at[j], r_e1.at[j], peer)
        c.start()
        sends.append(c)
    for j, (dz, da) in enumerate(SEVEN):
        block = eg.at[core, beta, lax.rem(zh + dz, 2), add4(alpha, 4 - da)]
        remote(block, block, s_e1.at[j], r_e1.at[j], seven_peers[j]).wait_recv()
    row = eg.at[core, beta]
    for k, peer in enumerate(beta_peers):
        c = remote(row, row, s_e2.at[k], r_e2.at[k], peer)
        c.start()
        sends.append(c)
    c = remote(row, row, s_e3.at[0], r_e3.at[0], partner)
    c.start()
    sends.append(c)
    for k in (1, 3, 2):
        block = eg.at[core, add4(beta, 4 - k)]
        remote(block, block, s_e2.at[k - 1], r_e2.at[k - 1], beta_peers[k - 1]).wait_recv()
        c = remote(block, block, s_e3.at[k], r_e3.at[k], partner)
        c.start()
        sends.append(c)

    def half_logits(ci):
        rows = eg[ci].reshape(R // 2, DX)
        left = rows[:, :D]

        def tile(t, _):
            cols = pl.ds(pl.multiple_of(t * CW, CW), CW)
            lb[:, cols] = jnp.dot(left, w_ref[:, cols], preferred_element_type=F32)
            return 0

        lax.fori_loop(0, W // CW, tile, 0)
        base = ci * (R // 2)

        def strip(i, _):
            here = pl.ds(pl.multiple_of(i * 32, 32), 32)
            there = pl.ds(pl.multiple_of(base + i * 32, 32), 32)
            v = lb[here, :] * LOGIT_SCALE
            m = jnp.max(v, axis=1, keepdims=True)
            p = jnp.exp(v - m)
            s = jnp.sum(p, axis=1, keepdims=True)
            pb[there, :] = p.astype(BF16)
            mcol[there, :] = jnp.broadcast_to(m, (32, 128))
            scol[there, :] = jnp.broadcast_to(s, (32, 128))
            return 0

        lax.fori_loop(0, R // 64, strip, 0)

    half_logits(core)
    obeta = alpha
    for k in (0, 1, 3, 2):
        block = eg.at[other, add4(obeta, 4 - k)]
        remote(block, block, s_e3.at[k], r_e3.at[k], partner).wait_recv()
    half_logits(other)
    for i in range(8):
        here = pl.ds(i * 128, 128)
        st[0, i : i + 1, :] = mcol[here, :].T[0:1, :]
        st[0, 8 + i : 9 + i, :] = scol[here, :].T[0:1, :]
    m_own = st[0, 0:8, :]

    def exchange(src, dst, ssem, rsem, peers):
        cs = [remote(src, dst.at[j], ssem.at[j], rsem.at[j], peer) for j, peer in enumerate(peers)]
        for c in cs:
            c.start()
        return cs

    def merge(src, dst, n):
        m = src[0:8, :]
        for j in range(n):
            m = jnp.maximum(m, dst[j, 0:8, :])
        s = src[8:16, :] * jnp.exp(src[0:8, :] - m)
        for j in range(n):
            s = s + dst[j, 8:16, :] * jnp.exp(dst[j, 0:8, :] - m)
        return m, s

    cs = exchange(st.at[0], ra, s_a.at[0], r_a.at[0], seven_peers)

    for ci in range(2):
        for b in range(4):
            blk = eg[ci, b].reshape(128, DX)
            at_row = (ci * 4 + b) * 128
            et[:, at_row : at_row + 128] = blk[:, :D].T
            d = blk[:, D:].astype(F32)
            icol[at_row : at_row + 128, :] = jnp.broadcast_to(
                d[:, 0:1] * 1024.0 + d[:, 1:2] * 32.0 + d[:, 2:3], (128, 128)
            )
    for c in cs:
        c.wait()
    m, s = merge(st.at[0], ra, 7)
    st[1, 0:8, :] = m
    st[1, 8:16, :] = s
    for c in (cs := exchange(st.at[1], rb, s_b.at[0], r_b.at[0], beta_peers)):
        c.wait()
    m, s = merge(st.at[1], rb, 3)
    st[2, 0:8, :] = m
    st[2, 8:16, :] = s
    for c in (cs := exchange(st.at[2], rc, s_c.at[0], r_c.at[0], [partner])):
        c.wait()
    m, s = merge(st.at[2], rc, 1)
    f = jnp.exp(m_own - m) / s

    frow = jnp.concatenate([f[i : i + 1, :] for i in range(8)], axis=1)
    fs = split_rows(frow)

    def mass(t, _):
        cols = pl.ds(pl.multiple_of(t * CW, CW), CW)
        part = jnp.dot(fs, pb[:, cols], preferred_element_type=F32)
        cm[0, :, cols] = jnp.sum(part, axis=0, keepdims=True)
        return 0

    lax.fori_loop(0, W // CW, mass, 0)
    cs = [remote(cm.at[0], cm.at[j], s_m.at[j - 1], r_m.at[j - 1], dp_peers[j - 1]) for j in (1, 2, 3)]
    for c in cs:
        c.start()
    for i in range(8):
        acol[i * 128 : (i + 1) * 128, :] = jnp.broadcast_to(f[i : i + 1, :], (128, 128)).T
    for c in cs:
        c.wait()
    lr = jnp.log((cm[0] + cm[1] + cm[2] + cm[3]) * classes_over_crops)

    ls = split_rows(lr)
    for h in range(2):
        part = lax.dot_general(ls, pb[h * 512 : (h + 1) * 512, :], NT, preferred_element_type=F32)
        part = jnp.sum(part, axis=0, keepdims=True)
        for i in range(4):
            k = h * 4 + i
            qt[0, k : k + 1, :] = part[:, i * 128 : (i + 1) * 128] * f[k : k + 1, :]
    for c in (cs := exchange(qt.at[0], qa, s_a.at[1], r_a.at[1], seven_peers)):
        c.wait()
    qt[1] = qt[0] + ((qa[0] + qa[1]) + (qa[2] + qa[3])) + ((qa[4] + qa[5]) + qa[6])
    for c in (cs := exchange(qt.at[1], qb, s_b.at[1], r_b.at[1], beta_peers)):
        c.wait()
    qt[2] = qt[1] + ((qb[0] + qb[1]) + qb[2])
    for c in (cs := exchange(qt.at[2], qc, s_c.at[1], r_c.at[1], [partner])):
        c.wait()
    rd = qt[2] + qc[0]
    cc = f * (1.0 - rd)
    for i in range(8):
        ccol[i * 128 : (i + 1) * 128, :] = jnp.broadcast_to(cc[i : i + 1, :], (128, 128)).T

    first_col = cls * W

    def chunk(t, _):
        cols = pl.ds(pl.multiple_of(t * CW, CW), CW)
        lrc = jnp.log((cm[0, :, cols] + cm[1, :, cols] + cm[2, :, cols] + cm[3, :, cols]) * classes_over_crops)
        ramp = (lax.broadcasted_iota(jnp.int32, (1, CW), 1) + (first_col + t * CW)).astype(F32)

        def strip(i, _):
            rows = pl.ds(pl.multiple_of(i * 32, 32), 32)
            a = acol[rows, 0:1]
            c = ccol[rows, 0:1]
            g = pb[rows, cols].astype(F32) * (a * lrc + c)
            g = g - (icol[rows, 0:1] == ramp).astype(F32)
            gb[rows, cols] = g.astype(BF16)
            return 0

        lax.fori_loop(0, R // 32, strip, 0)
        part = jnp.dot(et[...], gb[:, cols], preferred_element_type=F32) * LOGIT_SCALE
        for k in range(4):
            pf[t, k] = part[k * Q : (k + 1) * Q, :]
            pp[t, k] = part[k * Q : (k + 1) * Q, :].astype(BF16)
        for j in (1, 2, 3):
            remote(pp.at[t, add4(dp, j)], pr.at[t, j - 1], s_p.at[t, j - 1], r_p.at[t, j - 1], dp_peers[j - 1]).start()
        return 0

    lax.fori_loop(0, NC, chunk, 0)

    def half_embed(ci):
        def piece(b, _):
            rows = pl.ds(pl.multiple_of((ci * 4 + b) * 128, 128), 128)
            v = lax.dot_general(gb[rows, :], w_ref[...], NT, preferred_element_type=F32) * LOGIT_SCALE
            xe[ci, b] = v.reshape(2, 4, 16, D)
            return 0

        lax.fori_loop(0, 4, piece, 0)

    half_embed(other)
    c1 = remote(xe.at[other], xc, s_x1, r_x1, partner)
    c1.start()
    half_embed(core)
    c1.wait()
    xe[core] = xe[core] + xc[...]
    y1[...] = xe[core].astype(BF16)
    cs = [
        remote(y1.at[add4(beta, k)], xb.at[k - 1], s_x2.at[k - 1], r_x2.at[k - 1], beta_peers[k - 1])
        for k in (1, 2, 3)
    ]
    for c in cs:
        c.start()
    for c in cs:
        c.wait()
    own = xe[core, beta] + xb[0].astype(F32) + xb[1].astype(F32) + xb[2].astype(F32)
    xe[core, beta] = own
    y2[...] = own.astype(BF16)
    cs = []
    for j, (dz, da) in enumerate(SEVEN):
        z2, a2 = seven(dz, da)
        cs.append(remote(y2.at[z2, a2], xa.at[j], s_x3.at[j], r_x3.at[j], seven_peers[j]))
    for c in cs:
        c.start()

    for t in range(NC):
        for j in (1, 2, 3):
            remote(pp.at[t, add4(dp, j)], pr.at[t, j - 1], s_p.at[t, j - 1], r_p.at[t, j - 1], dp_peers[j - 1]).wait()
        po_ref[:, t * CW : (t + 1) * CW] = pf[t, dp] + (
            pr[t, 0].astype(F32) + pr[t, 1].astype(F32) + pr[t, 2].astype(F32)
        )
    for c in cs:
        c.wait()
    total = xe[core, beta, zh, alpha]
    for j in range(7):
        total = total + xa[j].astype(F32)
    eo_ref[...] = total
    for c in sends:
        c.wait_send()


def on_device(classes_over_crops, embeddings, cluster_ids, prototypes):
    vmem = pl.BlockSpec(memory_space=pltpu.VMEM)
    dma = pltpu.SemaphoreType.DMA
    V = pltpu.VMEM
    scratch = [
        V((2, 4, 2, 4, 16, DX), BF16),
        V((R, W), BF16),
        V((R // 2, W), F32),
        V((R, 128), F32),
        V((R, 128), F32),
        V((R, 128), F32),
        V((R, 128), F32),
        V((R, 128), F32),
        V((D, R), BF16),
        V((R, W), BF16),
        V((3, 16, 128), F32),
        V((7, 16, 128), F32),
        V((3, 16, 128), F32),
        V((1, 16, 128), F32),
        V((4, 1, W), F32),
        V((3, 8, 128), F32),
        V((7, 8, 128), F32),
        V((3, 8, 128), F32),
        V((1, 8, 128), F32),
        V((NC, 4, Q, CW), F32),
        V((NC, 4, Q, CW), BF16),
        V((NC, 3, Q, CW), BF16),
        V((2, 4, 2, 4, 16, D), F32),
        V((4, 2, 4, 16, D), F32),
        V((4, 2, 4, 16, D), BF16),
        V((3, 2, 4, 16, D), BF16),
        V((2, 4, 16, D), BF16),
        V((7, 16, D), BF16),
        dma((7,)), dma((7,)), dma((3,)), dma((3,)), dma((4,)), dma((4,)),
        dma((2, 7)), dma((2, 7)), dma((2, 3)), dma((2, 3)), dma((2, 1)), dma((2, 1)),
        dma((3,)), dma((3,)),
        dma((NC, 3)), dma((NC, 3)),
        dma, dma, dma((3,)), dma((3,)), dma((7,)), dma((7,)),
    ]
    return pl.pallas_call(
        functools.partial(kernel, classes_over_crops),
        out_shape=(jax.ShapeDtypeStruct((16, D), F32), jax.ShapeDtypeStruct((Q, W), F32)),
        in_specs=[vmem] * 3,
        out_specs=(vmem, vmem),
        scratch_shapes=scratch,
        compiler_params=pltpu.CompilerParams(
            collective_id=0, has_side_effects=True, vmem_limit_bytes=56 * 2**20
        ),
    )(embeddings, cluster_ids.reshape(16, 1), prototypes)


def solution(mesh):
    placed = (P(("dp", "cls"), None), P(("dp", "cls")), P(None, "cls"))
    return jax.shard_map(
        functools.partial(on_device, 131072 / 4096),
        mesh=mesh,
        in_specs=placed,
        out_specs=(P(("dp", "cls"), None), P("dp", "cls")),
        check_vma=False,
    )
```

time: 1020 us -> 108 us (0.11)
  blocking collectives: 747 us -> 0 us
  waiting for transfers between devices: 215 us -> 0 us
  Pallas kernels: 0 us -> 103 us
  other arithmetic: 19.2 us -> 0 us
  matrix products: 15.4 us -> 0 us
  between operations: 14.8 us -> 0.64 us
    psum x3 -> x0, blocking collectives: 411 us -> none  [the longest x1 201 us: on_device(): row_total = lax.psum(jnp.sum(exponent, axis=1), 'cls')]
    pmax x1 -> x0, blocking collectives: 201 us -> none  [on_device(): row_peak = lax.pmax(jnp.max(logits, axis=1), 'cls')]
    reduce_scatter x1 -> x0, waiting for transfers between devices: 151 us -> none  [on_device(): lax.psum_scatter(lax.dot_general(grad_narrow, prototypes, contract_cols,...]
    all_gather x1 -> x0, blocking collectives: 121 us -> none  [on_device(): lax.all_gather(embeddings, 'cls', axis=0, tiled=True)]
    pallas_call x0 -> x1, Pallas kernels: none -> 103 us  [on_device(): pl.pallas_call(functools.partial(kernel, classes_over_crops), out_shape=(...]
    unnamed x3 -> x0, waiting for transfers between devices: 63.8 us -> none
    dot_general x3 -> x0, matrix products: 15.4 us -> none  [the longest x1 6.25 us: on_device(): lax.dot_general(gathered, grad_narrow, contract_rows, preferred_element_t...]
    reduce_sum x3 -> x0, other arithmetic: 14.8 us -> none  [the longest x1 6.4 us: on_device(): column_mass = lax.psum(jnp.sum(soft_probs, axis=0), 'dp')]
  transfers between devices with their start and end apart: 2 -> 0, of which waited for: 2 -> 0; matrix products, arithmetic and copies ran while one was open for 1% -> 0% of each run, Pallas kernels for 0% -> 0%
where the time goes in v1:
time: 108 us
  Pallas kernels  103 us (95%)
  local copies, waits for them, and re-layouts  4.74 us (4%)
    pallas_call x1, Pallas kernels, on_device(): pl.pallas_call(functools.partial(kernel, classes_over_crops), out_shape=(...  103 us
    unnamed x2, local copies, waits for them, and re-layouts  3.41 us

profile of v1, /device:TPU:32, one launch (start us, length us, event | category | flops | bytes accessed | tf_op | source)
XLA Modules:
  0.0 108.0 jit_solution(14615078467834927743)
XLA Ops:
  0.6 1.3 %copy.5.id_ref = s32[16,1]{1,0:T(8,128)} copy(s32[16,1]{0,1:T(1,128)} %bitcast.1) | data formatting | bytes 128 | tf_op jit(solution)/shard_map/reshape | solution.py:357
  2.0 102.6 %shard_map.50 = (f32[16,384]{1,0:T(8,128)}, f32[96,2048]{1,0:T(8,128)}) custom-call(bf16[16,384]{1,0:T(8,128)(2,1)} %e_ref.1, s32[16,1]{1,0:T(8,128)} %copy.5.id_ref, bf16[384,2048]{1,0:T(8,128)(2,1)} %w_ref.1), custom_call_target="tpu_custom_call" | custom-call | tf_op jit(solution)/shard_map/pallas_call | solution.py:348
  104.6 1.3 %copy.8 = f32[16,384]{1,0:T(8,128)} copy(f32[16,384]{1,0:T(8,128)} %get-tuple-element.4) | data formatting | bytes 49152
  105.9 2.1 %copy.9 = f32[96,2048]{1,0:T(8,128)} copy(f32[96,2048]{1,0:T(8,128)} %get-tuple-element.5) | data formatting | bytes 1572864

commit v2 on v1

v2 whole, which is shorter than its diff:
```python
import functools

import jax
import jax.numpy as jnp
from jax import lax
from jax.experimental import pallas as pl
from jax.experimental.pallas import tpu as pltpu
from jax.sharding import PartitionSpec as P

LOGIT_SCALE = 10.0
MESH = pl.DeviceIdType.MESH
F32 = jnp.float32
BF16 = jnp.bfloat16

D = 384
DX = 512
W = 2048
R = 1024
H = W // 2
NC = 4
CW = H // NC
Q = D // 4
NT = (((1,), (1,)), ((), ()))
SEVEN = [(dz, da) for da in range(4) for dz in range(2) if dz or da]


def split_rows(v):
    hi = v.astype(BF16)
    r1 = v - hi.astype(F32)
    mid = r1.astype(BF16)
    lo = (r1 - mid.astype(F32)).astype(BF16)
    row = lax.broadcasted_iota(jnp.int32, (16, v.shape[1]), 0)
    zero = jnp.zeros((16, v.shape[1]), F32)
    out = jnp.where(row == 0, hi.astype(F32), zero)
    out = jnp.where(row == 1, mid.astype(F32), out)
    out = jnp.where(row == 2, lo.astype(F32), out)
    return out.astype(BF16)


def kernel(classes_over_crops, id_ref, e_ref, w_hbm, eo_ref, po_ref,
           w_ref, eg, eg2, pb, lb2, pb2, mcol, scol, acol, ccol, icol, acol2, ccol2, icol2, mcol2, et, et2, gb, gb2,
           st, ra, rb, rc, cm, lrow, lhalf, qt, qa, qb, qc, pf, pp, pr, ps, po2,
           xe, xc, y1, xb, y2, xa,
           s_w, s_e1, r_e1, s_e2, r_e2, s_e3, r_e3, s_f1, r_f1, s_f2, r_f2, s_f3, r_f3,
           s_a, r_a, s_b, r_b, s_c, r_c, s_m, r_m,
           s_po, r_po, s_pi, r_pi, s_ps, r_ps, s_x1, r_x1, s_x2, r_x2, s_x3, r_x3):
    dp = lax.axis_index("dp")
    cls = lax.axis_index("cls")
    core = lax.rem(cls, 2)
    x = lax.rem(cls // 2, 4)
    zh = lax.rem(cls // 8, 2)
    y = cls // 16
    other = 1 - core
    alpha = y * other + x * core
    beta = x * other + y * core
    pair = dp // 2
    mate = dp + 1 - 2 * lax.rem(dp, 2)
    inner = jnp.logical_or(dp == 1, dp == 2)
    far_in = 2 - pair
    far_out = 3 - 3 * pair
    own_cols = pair * H

    def at(zz, aa, bb):
        yy = aa * other + bb * core
        xx = bb * other + aa * core
        return (dp, ((yy * 2 + zz) * 4 + xx) * 2 + core)

    def add4(v, k):
        return lax.rem(v + k, 4)

    def seven(dz, da):
        return lax.rem(zh + dz, 2), add4(alpha, da)

    twin = cls + 1 - 2 * core
    partner = (dp, twin)
    buddy = add4(dp, 2)
    mate_peer = (mate, cls)
    pair_peers = [partner, (buddy, cls), (buddy, twin)]
    dp_peers = [(add4(dp, j), cls) for j in (1, 2, 3)]
    beta_peers = [at(zh, alpha, add4(beta, k)) for k in (1, 2, 3)]
    seven_peers = [at(*seven(dz, da), beta) for dz, da in SEVEN]

    barrier = pltpu.get_barrier_semaphore()
    everyone = [partner, (buddy, twin)] + dp_peers + beta_peers + seven_peers
    for peer in everyone:
        pl.semaphore_signal(barrier, inc=1, device_id=peer, device_id_type=MESH)
    load = pltpu.make_async_copy(w_hbm, w_ref, s_w)
    load.start()

    lane = lax.broadcasted_iota(jnp.int32, (16, 128), 1)
    line = lax.broadcasted_iota(jnp.int32, (16, 128), 0)
    ids = jnp.zeros((16, 128), jnp.int32)
    for i in range(16):
        ids = jnp.where(line == i, id_ref[i], ids)
    digits = jnp.where(lane == 0, ids >> 10, jnp.where(lane == 1, (ids >> 5) & 31, jnp.where(lane == 2, ids & 31, 0)))
    eg[core, beta, zh, alpha, :, :D] = e_ref[...]
    eg[core, beta, zh, alpha, :, D:] = digits.astype(F32).astype(BF16)

    pl.semaphore_wait(barrier, len(everyone))

    def remote(src, dst, ssem, rsem, peer):
        return pltpu.make_async_remote_copy(
            src_ref=src, dst_ref=dst, send_sem=ssem, recv_sem=rsem, device_id=peer, device_id_type=MESH
        )

    sends = []

    def post(src, dst, ssem, rsem, peer):
        c = remote(src, dst, ssem, rsem, peer)
        c.start()
        sends.append(c)

    mine = eg.at[core, beta, zh, alpha]
    for j, peer in enumerate(seven_peers):
        post(mine, mine, s_e1.at[j], r_e1.at[j], peer)
    for j, (dz, da) in enumerate(SEVEN):
        block = eg.at[core, beta, lax.rem(zh + dz, 2), add4(alpha, 4 - da)]
        remote(block, block, s_e1.at[j], r_e1.at[j], seven_peers[j]).wait_recv()
    row = eg.at[core, beta]
    for k, peer in enumerate(beta_peers):
        post(row, row, s_e2.at[k], r_e2.at[k], peer)
    post(row, row, s_e3.at[0], r_e3.at[0], partner)
    row2 = eg2.at[core, beta]
    post(row, row2, s_f1, r_f1, pair_peers[1])
    load.wait()
    for k in (1, 3, 2):
        b = add4(beta, 4 - k)
        block = eg.at[core, b]
        remote(block, block, s_e2.at[k - 1], r_e2.at[k - 1], beta_peers[k - 1]).wait_recv()
        post(block, block, s_e3.at[k], r_e3.at[k], partner)

    def half_logits(ci):
        for h in range(2):
            left = eg[ci, 2 * h : 2 * h + 2].reshape(256, DX)[:, :D]
            there = pl.ds(pl.multiple_of(ci * (R // 2) + h * 256, 256), 256)
            v = jnp.dot(left, w_ref[...], preferred_element_type=F32) * LOGIT_SCALE
            m = jnp.max(v, axis=1, keepdims=True)
            p = jnp.exp(v - m)
            s = jnp.sum(p, axis=1, keepdims=True)
            pb[there, :] = p.astype(BF16)
            mcol[there, :] = jnp.broadcast_to(m, (256, 128))
            scol[there, :] = jnp.broadcast_to(s, (256, 128))

    half_logits(core)
    for k in (0, 1, 3, 2):
        block = eg.at[other, add4(alpha, 4 - k)]
        remote(block, block, s_e3.at[k], r_e3.at[k], partner).wait_recv()
    half_logits(other)

    remote(row2, row2, s_f1, r_f1, pair_peers[1]).wait_recv()
    for k, peer in enumerate(beta_peers):
        post(row2, row2, s_f2.at[k], r_f2.at[k], peer)
    post(row2, row2, s_f3.at[0], r_f3.at[0], partner)

    eye = lax.broadcasted_iota(jnp.int32, (128, 128), 0) == lax.broadcasted_iota(jnp.int32, (128, 128), 1)

    def to_line(cols):
        return jnp.sum(jnp.where(eye, cols, 0.0), axis=0, keepdims=True)

    def to_cols(dst, lines):
        for i in range(8):
            dst[i * 128 : (i + 1) * 128, :] = jnp.broadcast_to(lines[i : i + 1, :], (128, 128)).T

    for i in range(8):
        here = pl.ds(i * 128, 128)
        st[0, i : i + 1, :] = to_line(mcol[here, :])
        st[0, 8 + i : 9 + i, :] = to_line(scol[here, :])

    def exchange(src, dst, ssem, rsem, peers):
        cs = [remote(src, dst.at[j], ssem.at[j], rsem.at[j], peer) for j, peer in enumerate(peers)]
        for c in cs:
            c.start()
        return cs

    def merge(parts):
        m = parts[0][0:8, :]
        for v in parts[1:]:
            m = jnp.maximum(m, v[0:8, :])
        s = parts[0][8:16, :] * jnp.exp(parts[0][0:8, :] - m)
        for v in parts[1:]:
            s = s + v[8:16, :] * jnp.exp(v[0:8, :] - m)
        return m, s

    cs = exchange(st.at[0], ra, s_a.at[0], r_a.at[0], seven_peers)

    for k in (1, 3, 2):
        block = eg2.at[core, add4(beta, 4 - k)]
        remote(block, block, s_f2.at[k - 1], r_f2.at[k - 1], beta_peers[k - 1]).wait_recv()
        post(block, block, s_f3.at[k], r_f3.at[k], partner)

    first_col = (cls * W).astype(F32)
    drow = lax.broadcasted_iota(jnp.int32, (128, 128), 0)
    weigh = jnp.where(drow == 0, 1024.0, jnp.where(drow == 1, 32.0, jnp.where(drow == 2, 1.0, 0.0))).astype(BF16)
    ramp = lax.broadcasted_iota(jnp.int32, (1, 128), 1).astype(F32)

    def turn(src, dst_t, dst_i, base):
        rows = src[...].reshape(R, DX)
        for i in range(8):
            dst_t[:, i * 128 : (i + 1) * 128] = rows[i * 128 : (i + 1) * 128, :D].T
        dst_i[...] = jnp.dot(rows[:, D:], weigh, preferred_element_type=F32) - (ramp + base)

    turn(eg, et, icol, first_col)
    for c in cs:
        c.wait()
    m, s = merge([st[0]] + [ra[j] for j in range(7)])
    st[1, 0:8, :] = m
    st[1, 8:16, :] = s
    cs = exchange(st.at[1], rb, s_b.at[0], r_b.at[0], beta_peers)

    for k in (0, 1, 3, 2):
        block = eg2.at[other, add4(alpha, 4 - k)]
        remote(block, block, s_f3.at[k], r_f3.at[k], partner).wait_recv()
    half_w = pl.ds(pl.multiple_of(own_cols, H), H)
    for h in range(2):
        left = eg2[h].reshape(R // 2, DX)[:, :D]
        lb2[h * 512 : (h + 1) * 512, :] = jnp.dot(left, w_ref[:, half_w], preferred_element_type=F32) * LOGIT_SCALE
    for c in cs:
        c.wait()
    m, s = merge([st[1]] + [rb[j] for j in range(3)])
    st[2, 0:8, :] = m
    st[2, 8:16, :] = s
    cs_stat = exchange(st.at[2], rc, s_c.at[0], r_c.at[0], pair_peers)
    cs_stat[0].wait()
    m, s = merge([st[2], rc[0]])
    f = jnp.exp(st[0, 0:8, :] - m) / s

    frow = jnp.concatenate([f[i : i + 1, :] for i in range(8)], axis=1)
    part = jnp.dot(split_rows(frow), pb[...], preferred_element_type=F32)
    cm[0] = jnp.sum(part, axis=0, keepdims=True)
    cs = [remote(cm.at[0], cm.at[j], s_m.at[j - 1], r_m.at[j - 1], dp_peers[j - 1]) for j in (1, 2, 3)]
    for c in cs:
        c.start()
    to_cols(acol, f)
    turn(eg2, et2, icol2, first_col + own_cols.astype(F32))
    for c in cs:
        c.wait()
    lr = jnp.log((cm[0] + cm[1] + cm[2] + cm[3]) * classes_over_crops)
    lrow[...] = lr
    lhalf[...] = lrow[:, half_w]

    part = lax.dot_general(split_rows(lr), pb[...], NT, preferred_element_type=F32)
    part = jnp.sum(part, axis=0, keepdims=True)
    for i in range(8):
        qt[0, i : i + 1, :] = part[:, i * 128 : (i + 1) * 128] * f[i : i + 1, :]
    cs = exchange(qt.at[0], qa, s_a.at[1], r_a.at[1], seven_peers)

    for c in cs_stat[1:]:
        c.wait()
    m2, s2 = merge([rc[1], rc[2]])
    to_cols(mcol2, m2)
    to_cols(acol2, 1.0 / s2)
    for i in range(4):
        rows = pl.ds(i * 256, 256)
        pb2[rows, :] = jnp.exp(lb2[rows, :] - mcol2[rows, 0:1]).astype(BF16)
    for c in cs:
        c.wait()
    qt[1] = qt[0] + ((qa[0] + qa[1]) + (qa[2] + qa[3])) + ((qa[4] + qa[5]) + qa[6])
    for c in (cs := exchange(qt.at[1], qb, s_b.at[1], r_b.at[1], beta_peers)):
        c.wait()
    qt[2] = qt[1] + ((qb[0] + qb[1]) + qb[2])
    cs_dot = exchange(qt.at[2], qc, s_c.at[1], r_c.at[1], pair_peers)
    cs_dot[0].wait()
    to_cols(ccol, f * (1.0 - (qt[2] + qc[0])))

    def grad(dst, src, a_ref, c_ref, i_ref, l_ref, width):
        def strip(i, _):
            rows = pl.ds(pl.multiple_of(i * 32, 32), 32)
            a = a_ref[rows, :]
            c = c_ref[rows, :]
            hit = i_ref[rows, :]
            for t in range(width // 128):
                cols = pl.ds(t * 128, 128)
                g = src[rows, cols].astype(F32) * (a * l_ref[:, cols] + c)
                g = jnp.where(hit == t * 128.0, g - 1.0, g)
                dst[rows, cols] = g.astype(BF16)
            return 0

        lax.fori_loop(0, R // 32, strip, 0)

    grad(gb, pb, acol, ccol, icol, lrow, W)

    def half_embed(ci):
        rows = pl.ds(pl.multiple_of(ci * 512, 512), 512)
        v = lax.dot_general(gb[rows, :], w_ref[...], NT, preferred_element_type=F32) * LOGIT_SCALE
        xe[ci] = v.reshape(4, 2, 4, 16, D)

    half_embed(other)
    c1 = remote(xe.at[other], xc, s_x1, r_x1, partner)
    c1.start()

    for c in cs_dot[1:]:
        c.wait()
    to_cols(ccol2, (1.0 - (qc[1] + qc[2])) / s2)
    grad(gb2, pb2, acol2, ccol2, icol2, lhalf, H)

    def outward(t):
        return remote(pp.at[t, pl.ds(0, 3)], pr.at[t], s_po.at[t], r_po.at[t], mate_peer)

    def inward(t):
        return remote(pp.at[t, 0], pr.at[t, 0], s_pi.at[t], r_pi.at[t], mate_peer)

    def proto(t):
        cols = pl.ds(pl.multiple_of(own_cols + t * CW, CW), CW)
        near = pl.ds(t * CW, CW)
        part = jnp.dot(et[...], gb[:, cols], preferred_element_type=F32)
        part = (part + jnp.dot(et2[...], gb2[:, near], preferred_element_type=F32)) * LOGIT_SCALE
        for k in range(4):
            pf[t, k] = part[k * Q : (k + 1) * Q, :]
        pp[t, 0] = pf[t, mate].astype(BF16)

        @pl.when(jnp.logical_not(inner))
        def _():
            pp[t, 1] = pf[t, far_in].astype(BF16)
            pp[t, 2] = pf[t, far_out].astype(BF16)
            outward(t).start()

        @pl.when(inner)
        def _():
            inward(t).start()

    proto(0)
    half_embed(core)
    c1.wait()
    xe[core] = xe[core] + xc[...]
    y1[...] = xe[core].astype(BF16)
    cs = [
        remote(y1.at[add4(beta, k)], xb.at[k - 1], s_x2.at[k - 1], r_x2.at[k - 1], beta_peers[k - 1])
        for k in (1, 2, 3)
    ]
    for c in cs:
        c.start()
    for t in range(1, NC):
        proto(t)

    def relay(t, j):
        peer = (far_in, cls) if j == 0 else (far_out, cls)
        return remote(ps.at[t, j], po2.at[t], s_ps.at[t, j], r_ps.at[t], peer)

    def settle(t):
        @pl.when(inner)
        def _():
            inward(t).wait_send()
            outward(t).wait_recv()
            ps[t, 1] = (pf[t, far_out] + pr[t, 2].astype(F32)).astype(BF16)
            relay(t, 1).start()
            ps[t, 0] = (pf[t, far_in] + pr[t, 1].astype(F32)).astype(BF16)
            relay(t, 0).start()

        @pl.when(jnp.logical_not(inner))
        def _():
            outward(t).wait_send()
            inward(t).wait_recv()

        cols = pl.ds(pl.multiple_of(own_cols + t * CW, CW), CW)
        po_ref[:, cols] = pf[t, dp] + pr[t, 0].astype(F32)

    settle(0)
    for c in cs:
        c.wait()
    own = xe[core, beta] + xb[0].astype(F32) + xb[1].astype(F32) + xb[2].astype(F32)
    xe[core, beta] = own
    y2[...] = own.astype(BF16)
    cs = []
    for j, (dz, da) in enumerate(SEVEN):
        z2, a2 = seven(dz, da)
        cs.append(remote(y2.at[z2, a2], xa.at[j], s_x3.at[j], r_x3.at[j], seven_peers[j]))
    for c in cs:
        c.start()
    for t in range(1, NC):
        settle(t)
    for c in cs:
        c.wait()
    total = xe[core, beta, zh, alpha]
    for j in range(7):
        total = total + xa[j].astype(F32)
    eo_ref[...] = total
    for t in range(NC):
        relay(t, 0).wait_recv()
        cols = pl.ds(pl.multiple_of(H - own_cols + t * CW, CW), CW)
        po_ref[:, cols] = po2[t].astype(F32)

    @pl.when(inner)
    def _():
        for t in range(NC):
            relay(t, 1).wait_send()
            relay(t, 0).wait_send()

    for c in sends:
        c.wait_send()


def on_device(classes_over_crops, embeddings, cluster_ids, prototypes):
    vmem = pl.BlockSpec(memory_space=pltpu.VMEM)
    dma = pltpu.SemaphoreType.DMA
    V = pltpu.VMEM
    scratch = [
        V((D, W), BF16),
        V((2, 4, 2, 4, 16, DX), BF16),
        V((2, 4, 2, 4, 16, DX), BF16),
        V((R, W), BF16),
        V((R, H), F32),
        V((R, H), BF16),
    ] + [V((R, 128), F32)] * 9 + [
        V((D, R), BF16),
        V((D, R), BF16),
        V((R, W), BF16),
        V((R, H), BF16),
        V((3, 16, 128), F32),
        V((7, 16, 128), F32),
        V((3, 16, 128), F32),
        V((3, 16, 128), F32),
        V((4, 1, W), F32),
        V((1, W), F32),
        V((1, H), F32),
        V((3, 8, 128), F32),
        V((7, 8, 128), F32),
        V((3, 8, 128), F32),
        V((3, 8, 128), F32),
        V((NC, 4, Q, CW), F32),
        V((NC, 3, Q, CW), BF16),
        V((NC, 3, Q, CW), BF16),
        V((NC, 2, Q, CW), BF16),
        V((NC, Q, CW), BF16),
        V((2, 4, 2, 4, 16, D), F32),
        V((4, 2, 4, 16, D), F32),
        V((4, 2, 4, 16, D), BF16),
        V((3, 2, 4, 16, D), BF16),
        V((2, 4, 16, D), BF16),
        V((7, 16, D), BF16),
        dma,
        dma((7,)), dma((7,)), dma((3,)), dma((3,)), dma((4,)), dma((4,)), dma, dma, dma((3,)), dma((3,)), dma((4,)), dma((4,)),
        dma((2, 7)), dma((2, 7)), dma((2, 3)), dma((2, 3)), dma((2, 3)), dma((2, 3)),
        dma((3,)), dma((3,)),
        dma((NC,)), dma((NC,)), dma((NC,)), dma((NC,)), dma((NC, 2)), dma((NC,)),
        dma, dma, dma((3,)), dma((3,)), dma((7,)), dma((7,)),
    ]
    return pl.pallas_call(
        functools.partial(kernel, classes_over_crops),
        out_shape=(jax.ShapeDtypeStruct((16, D), F32), jax.ShapeDtypeStruct((Q, W), F32)),
        in_specs=[pl.BlockSpec(memory_space=pltpu.SMEM), vmem, pl.BlockSpec(memory_space=pl.ANY)],
        out_specs=(vmem, vmem),
        scratch_shapes=scratch,
        compiler_params=pltpu.CompilerParams(
            collective_id=0, has_side_effects=True, vmem_limit_bytes=56 * 2**20
        ),
    )(cluster_ids, embeddings, prototypes)


def solution(mesh):
    placed = (P(("dp", "cls"), None), P(("dp", "cls")), P(None, "cls"))
    return jax.shard_map(
        functools.partial(on_device, 131072 / 4096),
        mesh=mesh,
        in_specs=placed,
        out_specs=(P(("dp", "cls"), None), P("dp", "cls")),
        check_vma=False,
    )
```

time: 108 us -> 87.1 us (0.81); the launches traced: 108 us -> 85.6 us
  Pallas kernels: 103 us -> 81.5 us
  local copies, waits for them, and re-layouts: 4.74 us -> 3.41 us
    pallas_call x1, Pallas kernels: 103 us -> 81.5 us  [on_device(): pl.pallas_call(functools.partial(kernel, classes_over_crops), out_shape=(...]
    reshape x1 -> x0, local copies, waits for them, and re-layouts: 1.33 us -> none  [on_device(): cluster_ids.reshape(16, 1)]
where the time goes in v2:
time: 87.1 us; the launch traced here: 85.6 us
  Pallas kernels  81.5 us (94%)
  local copies, waits for them, and re-layouts  3.41 us (4%)
    pallas_call x1, Pallas kernels, on_device(): pl.pallas_call(functools.partial(kernel, classes_over_crops), out_shape=(...  81.5 us
    unnamed x2, local copies, waits for them, and re-layouts  3.41 us

profile of v2, /device:TPU:32, one launch (start us, length us, event | category | flops | bytes accessed | tf_op | source)
XLA Modules:
  0.0 85.6 jit_solution(10921117794450482149)
XLA Ops:
  0.6 81.5 %shard_map.50 = (f32[16,384]{1,0:T(8,128)}, f32[96,2048]{1,0:T(8,128)}) custom-call(s32[16]{0:T(128)} %id_ref.1, bf16[16,384]{1,0:T(8,128)(2,1)} %e_ref.1, bf16[384,2048]{1,0:T(8,128)(2,1)} %w_hbm.1), custom_call_target="tpu_custom_call" | custom-call | tf_op jit(solution)/shard_map/pallas_call | solution.py:437
  82.2 1.3 %copy.7 = f32[16,384]{1,0:T(8,128)} copy(f32[16,384]{1,0:T(8,128)} %get-tuple-element.4) | data formatting | bytes 49152
  83.5 2.1 %copy.8 = f32[96,2048]{1,0:T(8,128)} copy(f32[96,2048]{1,0:T(8,128)} %get-tuple-element.5) | data formatting | bytes 1572864

commit v3 on v2

--- a/solution.py
+++ b/solution.py
@@ -39,11 +39,11 @@
 
 def kernel(classes_over_crops, id_ref, e_ref, w_hbm, eo_ref, po_ref,
            w_ref, eg, eg2, pb, lb2, pb2, mcol, scol, acol, ccol, icol, acol2, ccol2, icol2, mcol2, et, et2, gb, gb2,
-           st, ra, rb, rc, cm, lrow, lhalf, qt, qa, qb, qc, pf, pp, pr, ps, po2,
+           st, ra, rb, rc, cm, lrow, lhalf, qt, qa, qb, qc, pf, pp, pr, pn, rn, ps, po2,
            xe, xc, y1, xb, y2, xa,
            s_w, s_e1, r_e1, s_e2, r_e2, s_e3, r_e3, s_f1, r_f1, s_f2, r_f2, s_f3, r_f3,
            s_a, r_a, s_b, r_b, s_c, r_c, s_m, r_m,
-           s_po, r_po, s_pi, r_pi, s_ps, r_ps, s_x1, r_x1, s_x2, r_x2, s_x3, r_x3):
+           s_pf, r_pf, s_pn, r_pn, s_ps, r_ps, s_x1, r_x1, s_x2, r_x2, s_x3, r_x3):
     dp = lax.axis_index("dp")
     cls = lax.axis_index("cls")
     core = lax.rem(cls, 2)
@@ -75,13 +75,19 @@
     partner = (dp, twin)
     buddy = add4(dp, 2)
     mate_peer = (mate, cls)
-    pair_peers = [partner, (buddy, cls), (buddy, twin)]
+    buddy_peer = (buddy, cls)
     dp_peers = [(add4(dp, j), cls) for j in (1, 2, 3)]
     beta_peers = [at(zh, alpha, add4(beta, k)) for k in (1, 2, 3)]
     seven_peers = [at(*seven(dz, da), beta) for dz, da in SEVEN]
 
+    def cross(peer):
+        return (dp, peer[1] + 1 - 2 * core)
+
+    wide_peers = [partner] + beta_peers + [cross(p) for p in beta_peers]
+    wide_from = [cross(at(zh, add4(alpha, k), beta)) for k in (1, 2, 3)]
+
     barrier = pltpu.get_barrier_semaphore()
-    everyone = [partner, (buddy, twin)] + dp_peers + beta_peers + seven_peers
+    everyone = [partner] + dp_peers + beta_peers + seven_peers + wide_from
     for peer in everyone:
         pl.semaphore_signal(barrier, inc=1, device_id=peer, device_id_type=MESH)
     load = pltpu.make_async_copy(w_hbm, w_ref, s_w)
@@ -121,7 +127,7 @@
         post(row, row, s_e2.at[k], r_e2.at[k], peer)
     post(row, row, s_e3.at[0], r_e3.at[0], partner)
     row2 = eg2.at[core, beta]
-    post(row, row2, s_f1, r_f1, pair_peers[1])
+    post(row, row2, s_f1, r_f1, buddy_peer)
     load.wait()
     for k in (1, 3, 2):
         b = add4(beta, 4 - k)
@@ -147,7 +153,7 @@
         remote(block, block, s_e3.at[k], r_e3.at[k], partner).wait_recv()
     half_logits(other)
 
-    remote(row2, row2, s_f1, r_f1, pair_peers[1]).wait_recv()
+    remote(row2, row2, s_f1, r_f1, buddy_peer).wait_recv()
     for k, peer in enumerate(beta_peers):
         post(row2, row2, s_f2.at[k], r_f2.at[k], peer)
     post(row2, row2, s_f3.at[0], r_f3.at[0], partner)
@@ -205,7 +211,7 @@
     m, s = merge([st[0]] + [ra[j] for j in range(7)])
     st[1, 0:8, :] = m
     st[1, 8:16, :] = s
-    cs = exchange(st.at[1], rb, s_b.at[0], r_b.at[0], beta_peers)
+    cs = exchange(st.at[1], rb, s_b.at[0], r_b.at[0], wide_peers)
 
     for k in (0, 1, 3, 2):
         block = eg2.at[other, add4(alpha, 4 - k)]
@@ -216,12 +222,11 @@
         lb2[h * 512 : (h + 1) * 512, :] = jnp.dot(left, w_ref[:, half_w], preferred_element_type=F32) * LOGIT_SCALE
     for c in cs:
         c.wait()
-    m, s = merge([st[1]] + [rb[j] for j in range(3)])
+    m, s = merge([st[1]] + [rb[j] for j in range(7)])
     st[2, 0:8, :] = m
     st[2, 8:16, :] = s
-    cs_stat = exchange(st.at[2], rc, s_c.at[0], r_c.at[0], pair_peers)
-    cs_stat[0].wait()
-    m, s = merge([st[2], rc[0]])
+    to_buddy = remote(st.at[2], rc, s_c.at[0], r_c.at[0], buddy_peer)
+    to_buddy.start()
     f = jnp.exp(st[0, 0:8, :] - m) / s
 
     frow = jnp.concatenate([f[i : i + 1, :] for i in range(8)], axis=1)
@@ -244,31 +249,29 @@
         qt[0, i : i + 1, :] = part[:, i * 128 : (i + 1) * 128] * f[i : i + 1, :]
     cs = exchange(qt.at[0], qa, s_a.at[1], r_a.at[1], seven_peers)
 
-    for c in cs_stat[1:]:
-        c.wait()
-    m2, s2 = merge([rc[1], rc[2]])
-    to_cols(mcol2, m2)
-    to_cols(acol2, 1.0 / s2)
+    to_buddy.wait()
+    to_cols(mcol2, rc[0:8, :])
+    to_cols(acol2, 1.0 / rc[8:16, :])
     for i in range(4):
         rows = pl.ds(i * 256, 256)
         pb2[rows, :] = jnp.exp(lb2[rows, :] - mcol2[rows, 0:1]).astype(BF16)
     for c in cs:
         c.wait()
     qt[1] = qt[0] + ((qa[0] + qa[1]) + (qa[2] + qa[3])) + ((qa[4] + qa[5]) + qa[6])
-    for c in (cs := exchange(qt.at[1], qb, s_b.at[1], r_b.at[1], beta_peers)):
-        c.wait()
-    qt[2] = qt[1] + ((qb[0] + qb[1]) + qb[2])
-    cs_dot = exchange(qt.at[2], qc, s_c.at[1], r_c.at[1], pair_peers)
-    cs_dot[0].wait()
-    to_cols(ccol, f * (1.0 - (qt[2] + qc[0])))
-
-    def grad(dst, src, a_ref, c_ref, i_ref, l_ref, width):
+    for c in (cs := exchange(qt.at[1], qb, s_b.at[1], r_b.at[1], wide_peers)):
+        c.wait()
+    qt[2] = qt[1] + ((qb[0] + qb[1]) + (qb[2] + qb[3])) + ((qb[4] + qb[5]) + qb[6])
+    to_buddy = remote(qt.at[2], qc, s_c.at[1], r_c.at[1], buddy_peer)
+    to_buddy.start()
+    to_cols(ccol, f * (1.0 - qt[2]))
+
+    def grad(dst, src, a_ref, c_ref, i_ref, l_ref, first, width):
         def strip(i, _):
             rows = pl.ds(pl.multiple_of(i * 32, 32), 32)
             a = a_ref[rows, :]
             c = c_ref[rows, :]
             hit = i_ref[rows, :]
-            for t in range(width // 128):
+            for t in range(first // 128, (first + width) // 128):
                 cols = pl.ds(t * 128, 128)
                 g = src[rows, cols].astype(F32) * (a * l_ref[:, cols] + c)
                 g = jnp.where(hit == t * 128.0, g - 1.0, g)
@@ -277,48 +280,55 @@
 
         lax.fori_loop(0, R // 32, strip, 0)
 
-    grad(gb, pb, acol, ccol, icol, lrow, W)
-
     def half_embed(ci):
         rows = pl.ds(pl.multiple_of(ci * 512, 512), 512)
         v = lax.dot_general(gb[rows, :], w_ref[...], NT, preferred_element_type=F32) * LOGIT_SCALE
         xe[ci] = v.reshape(4, 2, 4, 16, D)
 
+    def far(t):
+        return remote(pp.at[t], pr.at[t], s_pf.at[t], r_pf.at[t], mate_peer)
+
+    def near(t):
+        return remote(pn.at[t], rn.at[t], s_pn.at[t], r_pn.at[t], mate_peer)
+
+    def relay(t, j):
+        peer = (far_in, cls) if j == 0 else (far_out, cls)
+        return remote(ps.at[t, j], po2.at[t], s_ps.at[t, j], r_ps.at[t], peer)
+
+    def proto(t):
+        cols = pl.ds(pl.multiple_of(own_cols + t * CW, CW), CW)
+        half = pl.ds(t * CW, CW)
+        part = jnp.dot(et[...], gb[:, cols], preferred_element_type=F32)
+        part = (part + jnp.dot(et2[...], gb2[:, half], preferred_element_type=F32)) * LOGIT_SCALE
+        for k in range(4):
+            pf[t, k] = part[k * Q : (k + 1) * Q, :]
+
+        @pl.when(jnp.logical_not(inner))
+        def _():
+            pp[t, 0] = pf[t, far_in].astype(BF16)
+            pp[t, 1] = pf[t, far_out].astype(BF16)
+            far(t).start()
+
+        pn[t] = pf[t, mate].astype(BF16)
+
+    def settle_far(t):
+        @pl.when(inner)
+        def _():
+            far(t).wait_recv()
+            ps[t, 1] = (pf[t, far_out] + pr[t, 1].astype(F32)).astype(BF16)
+            relay(t, 1).start()
+            ps[t, 0] = (pf[t, far_in] + pr[t, 0].astype(F32)).astype(BF16)
+            relay(t, 0).start()
+
+    grad(gb, pb, acol, ccol, icol, lrow, 0, W)
+    to_buddy.wait()
+    to_cols(ccol2, (1.0 - qc[...]) / rc[8:16, :])
+    grad(gb2, pb2, acol2, ccol2, icol2, lhalf, 0, H // 2)
+    proto(0)
     half_embed(other)
     c1 = remote(xe.at[other], xc, s_x1, r_x1, partner)
     c1.start()
-
-    for c in cs_dot[1:]:
-        c.wait()
-    to_cols(ccol2, (1.0 - (qc[1] + qc[2])) / s2)
-    grad(gb2, pb2, acol2, ccol2, icol2, lhalf, H)
-
-    def outward(t):
-        return remote(pp.at[t, pl.ds(0, 3)], pr.at[t], s_po.at[t], r_po.at[t], mate_peer)
-
-    def inward(t):
-        return remote(pp.at[t, 0], pr.at[t, 0], s_pi.at[t], r_pi.at[t], mate_peer)
-
-    def proto(t):
-        cols = pl.ds(pl.multiple_of(own_cols + t * CW, CW), CW)
-        near = pl.ds(t * CW, CW)
-        part = jnp.dot(et[...], gb[:, cols], preferred_element_type=F32)
-        part = (part + jnp.dot(et2[...], gb2[:, near], preferred_element_type=F32)) * LOGIT_SCALE
-        for k in range(4):
-            pf[t, k] = part[k * Q : (k + 1) * Q, :]
-        pp[t, 0] = pf[t, mate].astype(BF16)
-
-        @pl.when(jnp.logical_not(inner))
-        def _():
-            pp[t, 1] = pf[t, far_in].astype(BF16)
-            pp[t, 2] = pf[t, far_out].astype(BF16)
-            outward(t).start()
-
-        @pl.when(inner)
-        def _():
-            inward(t).start()
-
-    proto(0)
+    proto(1)
     half_embed(core)
     c1.wait()
     xe[core] = xe[core] + xc[...]
@@ -329,32 +339,13 @@
     ]
     for c in cs:
         c.start()
-    for t in range(1, NC):
-        proto(t)
-
-    def relay(t, j):
-        peer = (far_in, cls) if j == 0 else (far_out, cls)
-        return remote(ps.at[t, j], po2.at[t], s_ps.at[t, j], r_ps.at[t], peer)
-
-    def settle(t):
-        @pl.when(inner)
-        def _():
-            inward(t).wait_send()
-            outward(t).wait_recv()
-            ps[t, 1] = (pf[t, far_out] + pr[t, 2].astype(F32)).astype(BF16)
-            relay(t, 1).start()
-            ps[t, 0] = (pf[t, far_in] + pr[t, 1].astype(F32)).astype(BF16)
-            relay(t, 0).start()
-
-        @pl.when(jnp.logical_not(inner))
-        def _():
-            outward(t).wait_send()
-            inward(t).wait_recv()
-
-        cols = pl.ds(pl.multiple_of(own_cols + t * CW, CW), CW)
-        po_ref[:, cols] = pf[t, dp] + pr[t, 0].astype(F32)
-
-    settle(0)
+    grad(gb2, pb2, acol2, ccol2, icol2, lhalf, H // 2, H // 2)
+    proto(2)
+    proto(3)
+    for t in range(NC):
+        near(t).start()
+    settle_far(0)
+    settle_far(1)
     for c in cs:
         c.wait()
     own = xe[core, beta] + xb[0].astype(F32) + xb[1].astype(F32) + xb[2].astype(F32)
@@ -366,8 +357,12 @@
         cs.append(remote(y2.at[z2, a2], xa.at[j], s_x3.at[j], r_x3.at[j], seven_peers[j]))
     for c in cs:
         c.start()
-    for t in range(1, NC):
-        settle(t)
+    settle_far(2)
+    settle_far(3)
+    for t in range(NC):
+        near(t).wait()
+        cols = pl.ds(pl.multiple_of(own_cols + t * CW, CW), CW)
+        po_ref[:, cols] = pf[t, dp] + rn[t].astype(F32)
     for c in cs:
         c.wait()
     total = xe[core, beta, zh, alpha]
@@ -384,6 +379,11 @@
         for t in range(NC):
             relay(t, 1).wait_send()
             relay(t, 0).wait_send()
+
+    @pl.when(jnp.logical_not(inner))
+    def _():
+        for t in range(NC):
+            far(t).wait_send()
 
     for c in sends:
         c.wait_send()
@@ -407,18 +407,20 @@
         V((R, H), BF16),
         V((3, 16, 128), F32),
         V((7, 16, 128), F32),
-        V((3, 16, 128), F32),
-        V((3, 16, 128), F32),
+        V((7, 16, 128), F32),
+        V((16, 128), F32),
         V((4, 1, W), F32),
         V((1, W), F32),
         V((1, H), F32),
         V((3, 8, 128), F32),
         V((7, 8, 128), F32),
-        V((3, 8, 128), F32),
-        V((3, 8, 128), F32),
+        V((7, 8, 128), F32),
+        V((8, 128), F32),
         V((NC, 4, Q, CW), F32),
-        V((NC, 3, Q, CW), BF16),
-        V((NC, 3, Q, CW), BF16),
+        V((NC, 2, Q, CW), BF16),
+        V((NC, 2, Q, CW), BF16),
+        V((NC, Q, CW), BF16),
+        V((NC, Q, CW), BF16),
         V((NC, 2, Q, CW), BF16),
         V((NC, Q, CW), BF16),
         V((2, 4, 2, 4, 16, D), F32),
@@ -429,12 +431,12 @@
         V((7, 16, D), BF16),
         dma,
         dma((7,)), dma((7,)), dma((3,)), dma((3,)), dma((4,)), dma((4,)), dma, dma, dma((3,)), dma((3,)), dma((4,)), dma((4,)),
-        dma((2, 7)), dma((2, 7)), dma((2, 3)), dma((2, 3)), dma((2, 3)), dma((2, 3)),
+        dma((2, 7)), dma((2, 7)), dma((2, 7)), dma((2, 7)), dma((2,)), dma((2,)),
         dma((3,)), dma((3,)),
         dma((NC,)), dma((NC,)), dma((NC,)), dma((NC,)), dma((NC, 2)), dma((NC,)),
         dma, dma, dma((3,)), dma((3,)), dma((7,)), dma((7,)),
     ]
-    return pl.pallas_call(
+    halves = pl.pallas_call(
         functools.partial(kernel, classes_over_crops),
         out_shape=(jax.ShapeDtypeStruct((16, D), F32), jax.ShapeDtypeStruct((Q, W), F32)),
         in_specs=[pl.BlockSpec(memory_space=pltpu.SMEM), vmem, pl.BlockSpec(memory_space=pl.ANY)],
@@ -445,6 +447,20 @@
         ),
     )(cluster_ids, embeddings, prototypes)
 
+    any_space = pl.BlockSpec(memory_space=pl.ANY)
+
+    def hand_over(a_ref, b_ref, a_out, b_out, sems):
+        a_out[...] = a_ref[...]
+        b_out[...] = b_ref[...]
+
+    return pl.pallas_call(
+        hand_over,
+        out_shape=(jax.ShapeDtypeStruct((16, D), F32), jax.ShapeDtypeStruct((Q, W), F32)),
+        in_specs=[vmem] * 2,
+        out_specs=(vmem,) * 2,
+        scratch_shapes=[dma((2,))],
+    )(*halves)
+
 
 def solution(mesh):
     placed = (P(("dp", "cls"), None), P(("dp", "cls")), P(None, "cls"))

time: 87.1 us -> 83.7 us (0.961); the launches traced: 85.6 us -> 83.6 us
  local copies, waits for them, and re-layouts: 3.41 us -> 0 us
  Pallas kernels: 81.5 us -> 82.9 us
    unnamed x2 -> x0, local copies, waits for them, and re-layouts: 3.41 us -> none
    pallas_call x0 -> x1, Pallas kernels: none -> 2.1 us  [on_device(): pl.pallas_call(hand_over, out_shape=(jax.ShapeDtypeStruct((16, D), F32),...]
where the time goes in v3:
time: 83.7 us; the launch traced here: 83.6 us
  Pallas kernels  82.9 us (99%)
    pallas_call x1, Pallas kernels, on_device(): pl.pallas_call(functools.partial(kernel, classes_over_crops), out_shape=(...  80.8 us
    pallas_call x1, Pallas kernels, on_device(): pl.pallas_call(hand_over, out_shape=(jax.ShapeDtypeStruct((16, D), F32),...  2.1 us

profile of v3, /device:TPU:32, one launch (start us, length us, event | category | flops | bytes accessed | tf_op | source)
XLA Modules:
  0.0 83.6 jit_solution(5177171582041353863)
XLA Ops:
  0.6 80.8 %shard_map.50 = (f32[16,384]{1,0:T(8,128)}, f32[96,2048]{1,0:T(8,128)}) custom-call(s32[16]{0:T(128)} %id_ref.1, bf16[16,384]{1,0:T(8,128)(2,1)} %e_ref.1, bf16[384,2048]{1,0:T(8,128)(2,1)} %w_hbm.1), custom_call_target="tpu_custom_call" | custom-call | tf_op jit(solution)/shard_map/pallas_call | solution.py:439
  81.5 2.1 %shard_map.51 = (f32[16,384]{1,0:T(8,128)}, f32[96,2048]{1,0:T(8,128)}) custom-call(f32[16,384]{1,0:T(8,128)} %get-tuple-element.4.a_ref, f32[96,2048]{1,0:T(8,128)} %get-tuple-element.5.b_ref), custom_call_target="tpu_custom_call" | custom-call | tf_op jit(solution)/shard_map/pallas_call | solution.py:456

commit v4 on v3

--- a/solution.py
+++ b/solution.py
@@ -310,6 +310,7 @@
             far(t).start()
 
         pn[t] = pf[t, mate].astype(BF16)
+        near(t).start()
 
     def settle_far(t):
         @pl.when(inner)
@@ -325,10 +326,13 @@
     to_cols(ccol2, (1.0 - qc[...]) / rc[8:16, :])
     grad(gb2, pb2, acol2, ccol2, icol2, lhalf, 0, H // 2)
     proto(0)
+    proto(1)
     half_embed(other)
     c1 = remote(xe.at[other], xc, s_x1, r_x1, partner)
     c1.start()
-    proto(1)
+    grad(gb2, pb2, acol2, ccol2, icol2, lhalf, H // 2, H // 2)
+    proto(2)
+    proto(3)
     half_embed(core)
     c1.wait()
     xe[core] = xe[core] + xc[...]
@@ -339,11 +343,6 @@
     ]
     for c in cs:
         c.start()
-    grad(gb2, pb2, acol2, ccol2, icol2, lhalf, H // 2, H // 2)
-    proto(2)
-    proto(3)
-    for t in range(NC):
-        near(t).start()
     settle_far(0)
     settle_far(1)
     for c in cs:

time: 83.7 us -> 81 us (0.968)
  Pallas kernels: 82.9 us -> 80.1 us
    pallas_call x1, Pallas kernels: 80.8 us -> 78 us  [on_device(): pl.pallas_call(functools.partial(kernel, classes_over_crops), out_shape=(...]
where the time goes in v4:
time: 81 us; the launch traced here: 80.7 us
  Pallas kernels  80.1 us (99%)
    pallas_call x1, Pallas kernels, on_device(): pl.pallas_call(functools.partial(kernel, classes_over_crops), out_shape=(...  78 us
    pallas_call x1, Pallas kernels, on_device(): pl.pallas_call(hand_over, out_shape=(jax.ShapeDtypeStruct((16, D), F32),...  2.1 us

profile of v4, /device:TPU:32, one launch (start us, length us, event | category | flops | bytes accessed | tf_op | source)
XLA Modules:
  0.0 80.7 jit_solution(175870690788121422)
XLA Ops:
  0.6 78.0 %shard_map.50 = (f32[16,384]{1,0:T(8,128)}, f32[96,2048]{1,0:T(8,128)}) custom-call(s32[16]{0:T(128)} %id_ref.1, bf16[16,384]{1,0:T(8,128)(2,1)} %e_ref.1, bf16[384,2048]{1,0:T(8,128)(2,1)} %w_hbm.1), custom_call_target="tpu_custom_call" | custom-call | tf_op jit(solution)/shard_map/pallas_call | solution.py:438
  78.6 2.1 %shard_map.51 = (f32[16,384]{1,0:T(8,128)}, f32[96,2048]{1,0:T(8,128)}) custom-call(f32[16,384]{1,0:T(8,128)} %get-tuple-element.4.a_ref, f32[96,2048]{1,0:T(8,128)} %get-tuple-element.5.b_ref), custom_call_target="tpu_custom_call" | custom-call | tf_op jit(solution)/shard_map/pallas_call | solution.py:455

commit v5 on v4

--- a/solution.py
+++ b/solution.py
@@ -21,7 +21,7 @@
 CW = H // NC
 Q = D // 4
 NT = (((1,), (1,)), ((), ()))
-SEVEN = [(dz, da) for da in range(4) for dz in range(2) if dz or da]
+SEVEN = [(1, 2), (1, 1), (1, 3), (1, 0), (0, 2), (0, 1), (0, 3)]
 
 
 def split_rows(v):
@@ -83,11 +83,12 @@
     def cross(peer):
         return (dp, peer[1] + 1 - 2 * core)
 
-    wide_peers = [partner] + beta_peers + [cross(p) for p in beta_peers]
+    wide_peers = [cross(beta_peers[1]), beta_peers[1], cross(beta_peers[0]), cross(beta_peers[2])]
+    wide_peers = wide_peers + [beta_peers[0], beta_peers[2], partner]
     wide_from = [cross(at(zh, add4(alpha, k), beta)) for k in (1, 2, 3)]
 
     barrier = pltpu.get_barrier_semaphore()
-    everyone = [partner] + dp_peers + beta_peers + seven_peers + wide_from
+    everyone = seven_peers + dp_peers + wide_from + beta_peers + [partner]
     for peer in everyone:
         pl.semaphore_signal(barrier, inc=1, device_id=peer, device_id_type=MESH)
     load = pltpu.make_async_copy(w_hbm, w_ref, s_w)

time: 81 us -> 79.9 us (0.986)
  Pallas kernels: 80.1 us -> 78.8 us
    pallas_call x1, Pallas kernels: 78 us -> 76.7 us  [on_device(): pl.pallas_call(functools.partial(kernel, classes_over_crops), out_shape=(...]
where the time goes in v5:
time: 79.9 us; the launch traced here: 79.5 us
  Pallas kernels  78.8 us (99%)
    pallas_call x1, Pallas kernels, on_device(): pl.pallas_call(functools.partial(kernel, classes_over_crops), out_shape=(...  76.7 us
    pallas_call x1, Pallas kernels, on_device(): pl.pallas_call(hand_over, out_shape=(jax.ShapeDtypeStruct((16, D), F32),...  2.1 us

profile of v5, /device:TPU:32, one launch (start us, length us, event | category | flops | bytes accessed | tf_op | source)
XLA Modules:
  0.0 79.5 jit_solution(2306722811929498838)
XLA Ops:
  0.6 76.7 %shard_map.50 = (f32[16,384]{1,0:T(8,128)}, f32[96,2048]{1,0:T(8,128)}) custom-call(s32[16]{0:T(128)} %id_ref.1, bf16[16,384]{1,0:T(8,128)(2,1)} %e_ref.1, bf16[384,2048]{1,0:T(8,128)(2,1)} %w_hbm.1), custom_call_target="tpu_custom_call" | custom-call | tf_op jit(solution)/shard_map/pallas_call | solution.py:439
  77.4 2.1 %shard_map.51 = (f32[16,384]{1,0:T(8,128)}, f32[96,2048]{1,0:T(8,128)}) custom-call(f32[16,384]{1,0:T(8,128)} %get-tuple-element.4.a_ref, f32[96,2048]{1,0:T(8,128)} %get-tuple-element.5.b_ref), custom_call_target="tpu_custom_call" | custom-call | tf_op jit(solution)/shard_map/pallas_call | solution.py:456

commit v6 on v5

--- a/solution.py
+++ b/solution.py
@@ -124,8 +124,8 @@
         block = eg.at[core, beta, lax.rem(zh + dz, 2), add4(alpha, 4 - da)]
         remote(block, block, s_e1.at[j], r_e1.at[j], seven_peers[j]).wait_recv()
     row = eg.at[core, beta]
-    for k, peer in enumerate(beta_peers):
-        post(row, row, s_e2.at[k], r_e2.at[k], peer)
+    for k in (1, 0, 2):
+        post(row, row, s_e2.at[k], r_e2.at[k], beta_peers[k])
     post(row, row, s_e3.at[0], r_e3.at[0], partner)
     row2 = eg2.at[core, beta]
     post(row, row2, s_f1, r_f1, buddy_peer)
@@ -340,7 +340,7 @@
     y1[...] = xe[core].astype(BF16)
     cs = [
         remote(y1.at[add4(beta, k)], xb.at[k - 1], s_x2.at[k - 1], r_x2.at[k - 1], beta_peers[k - 1])
-        for k in (1, 2, 3)
+        for k in (2, 1, 3)
     ]
     for c in cs:
         c.start()

time: 79.9 us -> 80 us (level)
  no operation moved by 1% of the time
where the time goes in v6:
time: 80 us; the launch traced here: 79.2 us
  Pallas kernels  78.6 us (98%)
    pallas_call x1, Pallas kernels, on_device(): pl.pallas_call(functools.partial(kernel, classes_over_crops), out_shape=(...  76.5 us
    pallas_call x1, Pallas kernels, on_device(): pl.pallas_call(hand_over, out_shape=(jax.ShapeDtypeStruct((16, D), F32),...  2.1 us

profile of v6, /device:TPU:32, one launch (start us, length us, event | category | flops | bytes accessed | tf_op | source)
XLA Modules:
  0.0 79.2 jit_solution(3601699247342624582)
XLA Ops:
  0.6 76.5 %shard_map.50 = (f32[16,384]{1,0:T(8,128)}, f32[96,2048]{1,0:T(8,128)}) custom-call(s32[16]{0:T(128)} %id_ref.1, bf16[16,384]{1,0:T(8,128)(2,1)} %e_ref.1, bf16[384,2048]{1,0:T(8,128)(2,1)} %w_hbm.1), custom_call_target="tpu_custom_call" | custom-call | tf_op jit(solution)/shard_map/pallas_call | solution.py:439
  77.1 2.1 %shard_map.51 = (f32[16,384]{1,0:T(8,128)}, f32[96,2048]{1,0:T(8,128)}) custom-call(f32[16,384]{1,0:T(8,128)} %get-tuple-element.4.a_ref, f32[96,2048]{1,0:T(8,128)} %get-tuple-element.5.b_ref), custom_call_target="tpu_custom_call" | custom-call | tf_op jit(solution)/shard_map/pallas_call | solution.py:456
